TPU v7x, 512 devices: a whole 4x4x16 slice. The times are simulated.
512 devices in a mesh: ctx: 64 (over z_hi, x, y, core), head: 8 (over z_lo).
Axes of the slice: x: 4, y: 4, z: 16 (z_hi: 2, z_lo: 8; z = z_hi * 8 + z_lo), core: 2. Of those that a mesh axis runs over, the one named last changes fastest.
Arguments:
- q_nope: bfloat16 [2048, 8192], P('ctx', 'head'), may hold values from -4 to 4
- q_rope: bfloat16 [2048, 4096], P('ctx', 'head'), may hold values from -240 to 240
- prefix_latent: bfloat16 [2048, 512], P('ctx'), may hold values from -4 to 4
- prefix_rope: bfloat16 [2048, 64], P('ctx'), may hold values from -4 to 4
- group_latent: bfloat16 [2048, 512], P('ctx'), may hold values from -4 to 4
- group_rope: bfloat16 [2048, 64], P('ctx'), may hold values from -6 to 6
- lengths: int32 [64], P('ctx'), may hold values from 1 to 32, 1024 in all
- offset: int32 [1], replicated, may hold values from 0 to 4095
- w_uk: bfloat16 [64, 128, 512], P('head'), may hold values from -0.5 to 0.5
- w_uv: bfloat16 [64, 512, 128], P('head'), may hold values from -1 to 1
- w_out: bfloat16 [8192, 7168], P('head', 'ctx'), may hold values from -0.25 to 0.25
Outputs:
- mixed: bfloat16 [2048, 7168], P('head', 'ctx')
All inputs are finite; a program needn't handle non-finite values. No bound on the sum of `lengths` on one device may be relied on, other than what follows from the above.
Results may differ from a plain program's by a relative error of at most 0.02.
Values may be sent and summed in bfloat16 or wider, within the bound.
A program may use at most 64 MiB of HBM per device.

v0:
```python
import jax
import jax.numpy as jnp
from jax import lax
from jax.sharding import PartitionSpec as P

LAT = 512
ROPE = 64
NOPE = 128
VD = 128


def rotate(vectors, positions):
    half_width = vectors.shape[-1] // 2
    frequency = 10000.0 ** (-2.0 * jnp.arange(half_width, dtype=jnp.float32) / vectors.shape[-1])
    angles = positions[:, None] * frequency[None, :]
    shape_out = (angles.shape[0],) + (1,) * (vectors.ndim - 2) + (half_width,)
    cosine = jnp.cos(angles).reshape(shape_out)
    sine_part = jnp.sin(angles).reshape(shape_out)
    first_half = vectors[..., :half_width]
    second_half = vectors[..., half_width:]
    return jnp.concatenate(
        [
            first_half * cosine - second_half * sine_part,
            first_half * sine_part + second_half * cosine,
        ],
        axis=-1,
    )


def against(left_rows, right_rows):
    return lax.dot_general(
        left_rows, right_rows, (((1,), (1,)), ((), ())), preferred_element_type=jnp.float32
    )


def block_width(total, largest):
    width = min(largest, total)
    while total % width != 0:
        width = width - 1
    return width


def on_device(
    q_nope,
    q_rope,
    prefix_latent,
    prefix_rope,
    group_latent,
    group_rope,
    lengths,
    offset,
    w_uk,
    w_uv,
    w_out,
):
    tok_dev = q_nope.shape[0]
    h_dev = w_uk.shape[0]
    query_rows = tok_dev * h_dev
    score_scale = (NOPE + ROPE) ** (-0.5)
    first_token = lax.axis_index("ctx") * tok_dev
    positions = (offset[0] + first_token + jnp.arange(tok_dev, dtype=jnp.int32)).astype(jnp.float32)
    query_rot = (
        rotate(q_rope.reshape(tok_dev, h_dev, ROPE).astype(jnp.float32), positions)
        .astype(jnp.bfloat16)
        .reshape(query_rows, ROPE)
    )
    key_rot = rotate(group_rope.astype(jnp.float32), positions).astype(jnp.bfloat16)
    query_lat = jnp.einsum(
        "thn,hnl->thl",
        q_nope.reshape(tok_dev, h_dev, NOPE),
        w_uk,
        preferred_element_type=jnp.float32,
    )
    query_lat = query_lat.astype(jnp.bfloat16).reshape(query_rows, LAT)
    token_of_row = jnp.repeat(first_token + jnp.arange(tok_dev, dtype=jnp.int32), h_dev)
    row_flags = (jnp.arange(prefix_latent.shape[0], dtype=jnp.int32) < lengths[0]).astype(
        jnp.bfloat16
    )

    def accumulate(running, latent_part, rope_part, allowed):
        row_max, total_sum, accum = running
        scores = (against(query_lat, latent_part) + against(query_rot, rope_part)) * score_scale
        scores = jnp.where(allowed, scores, -1e30)
        new_max = jnp.maximum(row_max, jnp.max(scores, axis=1))
        weights = jnp.where(allowed, jnp.exp(scores - new_max[:, None]), 0.0)
        factor = jnp.exp(row_max - new_max)
        total_sum = total_sum * factor + jnp.sum(weights, axis=1)
        accum = accum * factor[:, None] + jnp.dot(
            weights.astype(jnp.bfloat16), latent_part, preferred_element_type=jnp.float32
        )
        return (new_max, total_sum, accum)

    all_latent, all_rope, all_flags = (
        lax.all_gather(prefix_latent, "ctx", axis=0, tiled=True),
        lax.all_gather(prefix_rope, "ctx", axis=0, tiled=True),
        lax.all_gather(row_flags, "ctx", axis=0, tiled=True),
    )
    new_latent, new_rope = (
        lax.all_gather(group_latent, "ctx", axis=0, tiled=True),
        lax.all_gather(key_rot, "ctx", axis=0, tiled=True),
    )
    prefix_total = all_latent.shape[0]
    prefix_block = block_width(prefix_total, 1024)
    prefix_count = prefix_total // prefix_block

    def prefix_step(running, pieces):
        latent_part, rope_part, flags = pieces
        allowed = jnp.broadcast_to(flags[None, :] > 0, (query_rows, flags.shape[0]))
        return (accumulate(running, latent_part, rope_part, allowed), None)

    starting = (
        jnp.full((query_rows,), -1e30, jnp.float32),
        jnp.zeros((query_rows,), jnp.float32),
        jnp.zeros((query_rows, LAT), jnp.float32),
    )
    running, unused = lax.scan(
        prefix_step,
        starting,
        (
            all_latent.reshape(prefix_count, prefix_block, LAT),
            all_rope.reshape(prefix_count, prefix_block, ROPE),
            all_flags.reshape(prefix_count, prefix_block),
        ),
    )
    group_total = new_latent.shape[0]
    group_block = block_width(group_total, 512)
    group_count = group_total // group_block

    def group_step(running, pieces):
        latent_part, rope_part, block_index = pieces
        first_row = block_index * group_block
        key_index = first_row + jnp.arange(group_block, dtype=jnp.int32)
        allowed = key_index[None, :] <= token_of_row[:, None]
        updated = accumulate(running, latent_part, rope_part, allowed)
        return (updated, None)

    running, unused = lax.scan(
        group_step,
        running,
        (
            new_latent.reshape(group_count, group_block, LAT),
            new_rope.reshape(group_count, group_block, ROPE),
            jnp.arange(group_count, dtype=jnp.int32),
        ),
    )
    row_max, total_sum, accum = running
    latent_out = (accum / total_sum[:, None]).astype(jnp.bfloat16).reshape(tok_dev, h_dev, LAT)
    values_out = jnp.einsum(
        "thl,hlv->thv", latent_out, w_uv, preferred_element_type=jnp.float32
    ).astype(jnp.bfloat16)
    values_out = values_out.reshape(tok_dev, h_dev * VD)
    partial_sums = jnp.dot(
        lax.all_gather(values_out, "ctx", axis=0, tiled=True),
        w_out,
        preferred_element_type=jnp.float32,
    )
    return lax.psum_scatter(
        partial_sums.astype(jnp.bfloat16), "head", scatter_dimension=0, tiled=True
    )


def solution(mesh):
    return jax.shard_map(
        on_device,
        mesh=mesh,
        in_specs=(
            P("ctx", "head"),
            P("ctx", "head"),
            P("ctx", None),
            P("ctx", None),
            P("ctx", None),
            P("ctx", None),
            P("ctx"),
            P(),
            P("head", None, None),
            P("head", None, None),
            P("head", "ctx"),
        ),
        out_specs=P("head", "ctx"),
        check_vma=False,
    )
```

profile of v0, /device:TPU:6, one launch (start us, length us, event | category | flops | bytes accessed | tf_op | source)
XLA Modules:
  0.0 841.1 jit_solution(16874207750196073536)
XLA Ops:
  12.2 1.3 dynamic-slice
  14.5 239.0 %all-reduce = bf16[2048]{0:T(1024)(128)(2,1)S(1)} all-reduce(bf16[2048]{0:T(1024)(128)(2,1)S(1)} %dynamic-update-slice), channel_id=1, replica_groups=mesh['ctx'=64,'head'=8] {'ctx'}, use_global_device_ids=true, to_apply=%add | all-reduce | flops 2048 | bytes 8192
  254.0 177.5 %all_gather.20 = bf16[2048,64]{1,0:T(8,128)(2,1)S(1)} all-gather(bf16[32,64]{1,0:T(8,128)(2,1)S(1)} %copy-done.3), channel_id=1, replica_groups=mesh['ctx'=64,'head'=8] {'ctx'}, dimensions={0}, use_global_device_ids=true | all-gather | bytes 266240 | tf_op jit(solution)/shard_map/all_gather | solution.py:95
  431.5 152.8 %all_gather.22 = bf16[2048,64]{1,0:T(8,128)(2,1)} all-gather(bf16[32,64]{1,0:T(8,128)(2,1)S(1)} %pad_maximum_fusion.1), channel_id=1, replica_groups=mesh['ctx'=64,'head'=8] {'ctx'}, dimensions={0}, use_global_device_ids=true | all-gather | bytes 266240 | tf_op jit(solution)/shard_map/all_gather | solution.py:100
  584.3 9.6 %while.31 = (s32[]{:T(128)}, f32[256]{0:T(256)S(1)}, f32[256]{0:T(256)S(1)}, f32[256,512]{1,0:T(8,128)S(1)}, bf16[2,1024]{1,0:T(2,128)(2,1)S(1)}, /*index=5*/bf1...) while((s32[]{:T(128)}, f32[256]{0:T(256)S(1)}, ...), condition=%wide.region_3.4_spmd.clone, body=%wide.region_0.3_spmd.clone.sunk | while | flops 573444352 | bytes 9002113 | solution.py:116
  584.3 1.7 fusion.94
  587.0 2.0 convolution_add_fusion.7
  589.1 1.7 fusion.94
  591.8 2.0 convolution_add_fusion.7
  593.9 23.1 %while.30 = (s32[]{:T(128)}, f32[256]{0:T(256)S(1)}, f32[256]{0:T(256)S(1)}, f32[256,512]{1,0:T(8,128)S(1)}, s32[4]{0:T(128)S(1)}, /*index=5*/bf16[4,512,512]{2,...) while((s32[]{:T(128)}, f32[256]{0:T(256)S(1)}, ...), condition=%wide.region_7.8_spmd.clone, body=%wide.region_4.7_spmd.clone.sunk | while | flops 287179776 | bytes 5177105 | solution.py:137
  595.2 1.4 fusion.86
  598.1 1.5 convolution_add_fusion.6
  601.0 1.4 fusion.86
  602.5 1.2 fusion.87
  603.9 1.5 convolution_add_fusion.6
  606.8 1.4 fusion.86
  608.3 1.2 fusion.87
  609.7 1.5 convolution_add_fusion.6
  612.5 1.4 fusion.86
  614.1 1.2 fusion.87
  615.4 1.5 convolution_add_fusion.6
  618.2 156.2 %all-gather.8.cloned.1.call-done = bf16[2048,1024]{1,0:T(8,128)(2,1)} async-done(((bf16[32,1024]{1,0:T(8,128)(2,1)}), bf16[2048,1024]{1,0:T(8,128)(2,1)}) %all-gather.8.cloned.1.call-update) | async-done | bytes 4194320 | tf_op jit(solution)/shard_map/all_gather | solution.py:153
  774.4 4.4 convolution_convert_fusion
  778.9 55.7 %reduce-scatter.2.cloned.1.call-done = bf16[256,112]{0,1:T(8,128)(2,1)} async-done(((bf16[2048,112]{0,1:T(8,128)(2,1)}), bf16[256,112]{0,1:T(8,128)(2,1)}) %reduce-scatter.2.cloned.1.call-update) | async-done | bytes 57360 | tf_op jit(solution)/shard_map/reduce_scatter | solution.py:157
  (85 shorter events, 13.3 us)
Async XLA Ops:
  6.5 3.8 copy-start
  6.5 247.5 %copy-start.3 = (bf16[32,64]{1,0:T(8,128)(2,1)S(1)}, bf16[32,64]{1,0:T(8,128)(2,1)}, u32[]{:S(2)}) copy-start(bf16[32,64]{1,0:T(8,128)(2,1)} %param.18) | copy-start | bytes 12292
  6.5 577.8 %all-gather.4.cloned.1.call-start = ((), (), s32[]{:S(2)}) async-start(), calls=%async_computation.1 | async-start | bytes 2129920 | tf_op jit(solution)/shard_map/all_gather | solution.py:94
  7.3 586.6 %all-gather.6.cloned.1.call-start = ((), (), s32[]{:S(2)}) async-start(), calls=%async_computation.2 | async-start | bytes 2129920 | tf_op jit(solution)/shard_map/all_gather | solution.py:99
  8.0 766.4 %all-gather.8.cloned.1.call-start = ((), (), s32[]{:S(2)}) async-start(), calls=%async_computation.3 | async-start | bytes 4259840 | tf_op jit(solution)/shard_map/all_gather | solution.py:153
  593.9 23.2 %copy-start.1 = (bf16[8,512,128]{2,1,0:T(8,128)(2,1)S(1)}, bf16[8,512,128]{2,1,0:T(8,128)(2,1)}, u32[]{:S(2)}) copy-start(bf16[8,512,128]{2,1,0:T(8,128)(2,1)} %param.24) | copy-start | bytes 3145732
  617.0 157.4 %copy-start.2 = (bf16[1024,112]{0,1:T(8,128)(2,1)S(1)}, bf16[1024,112]{0,1:T(8,128)(2,1)}, u32[]{:S(2)}) copy-start(bf16[1024,112]{0,1:T(8,128)(2,1)} %param.25) | copy-start | bytes 688132
  618.1 216.4 %reduce-scatter.2.cloned.1.call-start = ((), (), s32[]{:S(2)}) async-start(), calls=%async_computation.4 | async-start | bytes 516096 | tf_op jit(solution)/shard_map/reduce_scatter | solution.py:157
Sparse Core Ops, SparseCore 0:
  11.8 115.4 all-gather.3
  131.8 101.9 all-gather.5
  618.2 156.1 all-gather.7
  779.0 55.5 reduce-scatter.1
where the time goes:
time: 842 us; the launch traced here: 841 us
  blocking collectives  569 us (68%)
  waiting for transfers between devices  213 us (25%)
  matrix products  31.2 us (4%)
  between operations  15.3 us (2%)
    unnamed x1, blocking collectives  239 us
    all_gather x1, blocking collectives, on_device(): lax.all_gather(prefix_rope, 'ctx', axis=0, tiled=True)  177 us
    all_gather x1, waiting for transfers between devices, on_device(): lax.all_gather(values_out, 'ctx', axis=0, tiled=True)  156 us
    all_gather x1, blocking collectives, on_device(): lax.all_gather(key_rot, 'ctx', axis=0, tiled=True)  153 us
    reduce_scatter x1, waiting for transfers between devices, on_device(): lax.psum_scatter(partial_sums.astype(jnp.bfloat16), 'head', scatter_dimen...  55.7 us
  transfers between devices with their start and end apart: 4, of which 2 were waited for; matrix products, arithmetic and copies ran while one was open for 2% of the time, Pallas kernels for 0%

commit v1 on v0

v1 whole, which is shorter than its diff:
```python
import functools
import math

import jax
import jax.numpy as jnp
import numpy as np
from jax import lax
from jax.experimental import pallas as pl
from jax.experimental.pallas import tpu as pltpu
from jax.sharding import PartitionSpec as P

ROPE = 64
NOPE = 128
VD = 128
NX = 4
NY = 4
HIDDEN = -1e30
MESH = pl.DeviceIdType.MESH


class Place:
    def __init__(self, heads):
        c = lax.axis_index("ctx")
        self.heads = heads
        self.head = lax.axis_index("head")
        self.core = lax.rem(c, 2)
        self.y = lax.rem(lax.div(c, 2), NY)
        self.x = lax.rem(lax.div(c, 2 * NY), NX)
        self.zh = lax.div(c, 2 * NX * NY)

    def ctx(self, zh=None, x=None, y=None, core=None):
        zh = self.zh if zh is None else zh
        x = self.x if x is None else x
        y = self.y if y is None else y
        core = self.core if core is None else core
        return ((zh * NX + x) * NY + y) * 2 + core

    def along(self, axis, step):
        if axis == 0:
            return (self.ctx(x=lax.rem(self.x + step + NX, NX)), self.head)
        return (self.ctx(y=lax.rem(self.y + step + NY, NY)), self.head)

    def sibling(self):
        return (self.ctx(core=1 - self.core), self.head)

    def across(self, head=None):
        return (self.ctx(zh=1 - self.zh), self.head if head is None else head)


    def up(self, step):
        z = lax.rem(self.zh * self.heads + self.head + step + 2 * self.heads, 2 * self.heads)
        return lax.div(z, self.heads), lax.rem(z, self.heads)


def greet(devices):
    barrier = pltpu.get_barrier_semaphore()
    for device in devices:
        pl.semaphore_signal(barrier, inc=1, device_id=device, device_id_type=MESH)


def plane_peers(place):
    return [place.along(axis, step) for axis in (0, 1) for step in (1, -1, 2)] + [place.sibling()]


RING = 16
OFFSETS = (0, -1, 1, 2)
STEPS = (1, -1, 2)


class Gather:
    def __init__(self, place, buf, ring_send, ring_recv, pair_send, pair_recv):
        self.place = place
        self.buf = buf
        self.ring_send, self.ring_recv = ring_send, ring_recv
        self.pair_send, self.pair_recv = pair_send, pair_recv

    def zh(self, plane):
        return self.place.zh if plane == 0 else 1 - self.place.zh

    def cell(self, kind, plane, first, second):
        place = self.place
        dx, dy = (second, first) if kind == 0 else (first, second)
        x = lax.rem(place.x + dx + NX, NX)
        y = lax.rem(place.y + dy + NY, NY)
        return self.buf.at[kind, self.zh(plane), x, y, place.core]

    def line(self, kind, plane, second):
        place, zh = self.place, self.zh(plane)
        if kind == 0:
            return self.buf.at[kind, zh, lax.rem(place.x + second + NX, NX), pl.ds(0, NY), place.core]
        return self.buf.at[kind, zh, pl.ds(0, NX), lax.rem(place.y + second + NY, NY), place.core]

    def copy(self, ref, kind, plane, slot, device):
        index = (kind * 2 + plane) * RING + slot
        return pltpu.make_async_remote_copy(
            src_ref=ref,
            dst_ref=ref,
            send_sem=self.ring_send.at[index],
            recv_sem=self.ring_recv.at[index],
            device_id=device,
            device_id_type=MESH,
        )

    def first(self, kind, plane, i):
        return self.copy(self.cell(kind, plane, 0, 0), kind, plane, i, self.place.along(1 - kind, STEPS[i]))

    def second(self, kind, plane, o, direction):
        ref = self.cell(kind, plane, OFFSETS[o], 0)
        return self.copy(ref, kind, plane, 3 + 2 * o + direction, self.place.along(kind, STEPS[direction]))

    def relay(self, kind, plane, o):
        direction = o // 2
        ref = self.cell(kind, plane, OFFSETS[o], -STEPS[direction])
        return self.copy(ref, kind, plane, 11 + o, self.place.along(kind, STEPS[direction]))

    def pair(self, kind, plane, piece):
        ref = self.line(kind, plane, OFFSETS[piece])
        index = (kind * 2 + plane) * 4 + piece
        return pltpu.make_async_remote_copy(
            src_ref=ref,
            dst_ref=ref,
            send_sem=self.pair_send.at[index],
            recv_sem=self.pair_recv.at[index],
            device_id=self.place.sibling(),
            device_id_type=MESH,
        )

    def start(self, plane):
        for i in range(3):
            for kind in (0, 1):
                self.first(kind, plane, i).start()
        for direction in (0, 1):
            for kind in (0, 1):
                self.second(kind, plane, 0, direction).start()

    def spread(self, plane):
        for i in range(3):
            for kind in (0, 1):
                self.first(kind, plane, i).wait_recv()
                for direction in (0, 1):
                    self.second(kind, plane, 1 + i, direction).start()
        for kind in (0, 1):
            self.pair(kind, plane, 0).start()

    def hand_on(self, plane):
        for o in range(4):
            for kind in (0, 1):
                for direction in (0, 1):
                    self.second(kind, plane, o, direction).wait_recv()
                self.relay(kind, plane, o).start()
        for piece in (1, 2):
            for kind in (0, 1):
                self.pair(kind, plane, piece).start()

    def complete(self, plane):
        for kind in (0, 1):
            for o in range(4):
                self.relay(kind, plane, o).wait_recv()
            self.pair(kind, plane, 3).start()

    def from_sibling(self, plane):
        for kind in (0, 1):
            for piece in range(4):
                self.pair(kind, plane, piece).wait_recv()

    def finish(self, plane):
        for kind in (0, 1):
            for i in range(3):
                self.first(kind, plane, i).wait_send()
            for o in range(4):
                for direction in (0, 1):
                    self.second(kind, plane, o, direction).wait_send()
                self.relay(kind, plane, o).wait_send()
                self.pair(kind, plane, o).wait_send()


def last_dims(a, b):
    return lax.dot_general(a, b, (((1,), (1,)), ((), ())), preferred_element_type=jnp.float32)


def cos_sin(angle):
    turns = jnp.floor(angle * (2.0 / math.pi) + 0.5)
    rest = ((angle - turns * 1.5703125) - turns * 4.837512969970703125e-4) - turns * 7.54978995489188216e-8
    square = rest * rest
    sine = ((-1.9515295891e-4 * square + 8.3321608736e-3) * square - 1.6666654611e-1) * square * rest + rest
    cosine = (2.443315711809948e-5 * square - 1.388731625493765e-3) * square + 4.166664568298827e-2
    cosine = cosine * square * square - 0.5 * square + 1.0
    quarter = jnp.bitwise_and(turns.astype(jnp.int32), 3)
    swap = jnp.bitwise_and(quarter, 1) == 1
    cos_part = jnp.where(swap, sine, cosine)
    sin_part = jnp.where(swap, cosine, sine)
    cos_part = jnp.where(jnp.logical_or(quarter == 1, quarter == 2), -cos_part, cos_part)
    sin_part = jnp.where(quarter >= 2, -sin_part, sin_part)
    return cos_part, sin_part


def kernel(
    heads,
    lengths,
    offset,
    q_nope_any,
    q_rope_any,
    prefix_latent,
    prefix_rope_any,
    group_latent,
    group_rope_any,
    frequency_any,
    w_uk_any,
    w_uv_any,
    w_out_any,
    mixed,
    keys,
    query,
    row_max,
    row_sum,
    accum,
    outs,
    staged,
    passing,
    w_out,
    shares,
    arrived,
    q_nope,
    q_rope,
    prefix_rope,
    group_rope,
    w_uk,
    w_uv,
    frequency,
    load_sem,
    k_ring_send,
    k_ring_recv,
    k_pair_send,
    k_pair_recv,
    k_cross_send,
    k_cross_recv,
    o_ring_send,
    o_ring_recv,
    o_pair_send,
    o_pair_recv,
    leg_send,
    leg_recv,
    o_cross_send,
    o_cross_recv,
    swap_send,
    swap_recv,
    w_send,
    w_recv,
    share_send,
    share_recv,
):
    place = Place(heads)
    rows, lat = prefix_latent.shape
    h_dev = w_uk.shape[0]
    width = keys.shape[-1]
    half = staged.shape[-1]
    half_heads = heads // 2
    me = place.ctx()
    own = (place.zh, place.x, place.y, place.core)
    odd = lax.rem(place.head, 2)
    paired = place.head + 1 - 2 * odd
    stays = place.core == odd
    moves = place.core != odd
    is_end = jnp.logical_or(place.head == 0, place.head == heads - 1)

    quarter = heads // 2
    legs = []
    for step in (quarter, -quarter):
        leg_zh, leg_head = place.up(step)
        legs.append((place.ctx(zh=leg_zh), leg_head))
    swap_device = (place.ctx(core=1 - place.core), paired)
    swap_across = (place.ctx(zh=1 - place.zh, core=1 - place.core), paired)
    others = [(me, lax.rem(place.head + j, heads)) for j in range(1, heads)]
    far_end = jnp.where(place.head < half_heads, heads - 1, 0)
    served = [jnp.where(place.head == 0, heads - 1 - j, j) for j in range(half_heads)]
    peers = plane_peers(place) + others + [place.across(far_end)]

    greet(peers)

    @pl.when(stays)
    def _():
        greet(legs)

    @pl.when(moves)
    def _():
        greet([swap_device, swap_across])

    @pl.when(is_end)
    def _():
        greet([place.across(head) for head in served])

    loads = [
        pltpu.make_async_copy(src, dst, load_sem.at[i])
        for i, (src, dst) in enumerate(
            (
                (prefix_latent, keys.at[(0,) + own + (slice(None), pl.ds(0, lat))]),
                (group_latent, keys.at[(1,) + own + (slice(None), pl.ds(0, lat))]),
                (q_nope_any, q_nope),
                (q_rope_any, q_rope),
                (prefix_rope_any, prefix_rope),
                (group_rope_any, group_rope),
                (w_uk_any, w_uk),
                (w_uv_any, w_uv),
                (w_out_any, w_out.at[odd]),
                (frequency_any, frequency),
            )
        )
    ]
    for load in loads:
        load.start()
    lane = lax.broadcasted_iota(jnp.int32, (rows, 128), 1)
    row = lax.broadcasted_iota(jnp.int32, (rows, 128), 0)
    for i in (9, 4, 5):
        loads[i].wait()
    positions = (offset[0] + me * rows + row).astype(jnp.float32)
    cos_part, sin_part = cos_sin(positions * frequency[...])
    first_half = lax.rem(lane, ROPE) < ROPE // 2
    sin_part = jnp.where(first_half, -sin_part, sin_part)

    def turn(tile):
        swapped = jnp.where(first_half, pltpu.roll(tile, 128 - ROPE // 2, 1), pltpu.roll(tile, ROPE // 2, 1))
        return tile * cos_part + swapped * sin_part

    def twice(ref):
        value = ref[...].astype(jnp.float32)
        return jnp.concatenate([value, value], axis=1)

    flags = jnp.where(jnp.logical_and(lane == ROPE, row >= lengths[0]), HIDDEN, 0.0)
    tail = pl.ds(lat, width - lat)
    keys[(0,) + own + (slice(None), tail)] = jnp.where(lane < ROPE, twice(prefix_rope), flags).astype(jnp.bfloat16)
    keys[(1,) + own + (slice(None), tail)] = jnp.where(lane < ROPE, turn(twice(group_rope)), 0.0).astype(jnp.bfloat16)
    loads[0].wait()
    loads[1].wait()

    pl.semaphore_wait(pltpu.get_barrier_semaphore(), len(peers) + 2 + half_heads * is_end.astype(jnp.int32))

    gather = Gather(place, keys, k_ring_send, k_ring_recv, k_pair_send, k_pair_recv)

    def key_cross(kind, j):
        ref = keys.at[(kind,) + own]
        return pltpu.make_async_remote_copy(
            src_ref=ref,
            dst_ref=ref,
            send_sem=k_cross_send.at[kind * half_heads + j],
            recv_sem=k_cross_recv.at[kind],
            device_id=place.across(served[j]),
            device_id_type=MESH,
        )

    @pl.when(is_end)
    def _():
        for j in reversed(range(half_heads)):
            for kind in (0, 1):
                key_cross(kind, j).start()

    gather.start(0)

    loads[2].wait()
    loads[3].wait()
    loads[6].wait()
    one = jnp.where(lane == ROPE, 1.0, 0.0)
    for pair in range(h_dev // 2):
        tile = q_rope[:, pair * 128 : (pair + 1) * 128].astype(jnp.float32)
        turned = turn(tile)
        for side in (0, 1):
            head = 2 * pair + side
            if side == 1:
                turned = pltpu.roll(turned, ROPE, 1)
            query[pl.ds(head * rows, rows), pl.ds(lat, width - lat)] = jnp.where(lane < ROPE, turned, one).astype(
                jnp.bfloat16
            )
            query[pl.ds(head * rows, rows), pl.ds(0, lat)] = jnp.dot(
                q_nope[:, head * NOPE : (head + 1) * NOPE], w_uk[head], preferred_element_type=jnp.float32
            ).astype(jnp.bfloat16)

    row_max[...] = jnp.full(row_max.shape, HIDDEN, jnp.float32)
    row_sum[...] = jnp.zeros(row_sum.shape, jnp.float32)
    accum[...] = jnp.zeros(accum.shape, jnp.float32)
    scale = (NOPE + ROPE) ** -0.5 * math.log2(math.e)
    q_rows = h_dev * rows
    chunk = NX * NY * rows
    my_token = me * rows + lax.rem(lax.broadcasted_iota(jnp.int32, (q_rows, 1), 0), rows)

    def attend(kind, zh, core):
        part = keys[kind, zh, :, :, core].reshape(chunk, width)
        scores = last_dims(query[...], part) * scale
        if kind == 1:
            index = lax.broadcasted_iota(jnp.int32, (1, chunk), 1)
            place_of = (zh * NX * NY + lax.div(index, rows)) * 2 + core
            key_token = place_of * rows + lax.rem(index, rows)
            scores = jnp.where(key_token <= my_token, scores, HIDDEN)
        old_max = row_max[...]
        new_max = jnp.maximum(old_max, jnp.max(scores, axis=1, keepdims=True))
        weights = jnp.exp2(scores - new_max)
        factor = jnp.exp2(old_max - new_max)
        row_max[...] = new_max
        row_sum[...] = row_sum[...] * factor + jnp.sum(weights, axis=1, keepdims=True)
        accum[...] = accum[...] * factor + jnp.dot(
            weights.astype(jnp.bfloat16), part[:, :lat], preferred_element_type=jnp.float32
        )

    w_copy = pltpu.make_async_remote_copy(
        src_ref=w_out_any,
        dst_ref=w_out.at[odd],
        send_sem=w_send,
        recv_sem=w_recv,
        device_id=(me, paired),
        device_id_type=MESH,
    )

    gather.spread(0)
    gather.hand_on(0)
    for kind in (0, 1):
        key_cross(kind, 0).wait_recv()
    gather.start(1)
    w_copy.start()
    gather.complete(0)
    gather.spread(1)
    attend(0, place.zh, place.core)
    gather.hand_on(1)
    attend(1, place.zh, place.core)
    gather.from_sibling(0)
    attend(0, place.zh, 1 - place.core)
    gather.complete(1)
    attend(1, place.zh, 1 - place.core)
    attend(0, 1 - place.zh, place.core)
    attend(1, 1 - place.zh, place.core)
    gather.from_sibling(1)
    attend(0, 1 - place.zh, 1 - place.core)
    attend(1, 1 - place.zh, 1 - place.core)

    loads[7].wait()
    latent_out = (accum[...] / row_sum[...]).astype(jnp.bfloat16)
    per_kind = half // VD
    for head in range(h_dev):
        staged[head // per_kind, :, pl.ds((head % per_kind) * VD, VD)] = jnp.dot(
            latent_out[head * rows : (head + 1) * rows], w_uv[head], preferred_element_type=jnp.float32
        ).astype(jnp.bfloat16)

    slot = (place.x, place.y, place.core)
    new_slot = (place.x, place.y, 1 - place.core)

    def leg(kind):
        return pltpu.make_async_remote_copy(
            src_ref=staged.at[kind],
            dst_ref=passing.at[kind],
            send_sem=leg_send.at[kind],
            recv_sem=leg_recv.at[kind],
            device_id=legs[kind],
            device_id_type=MESH,
        )

    def second_leg(kind):
        end_zh = place.up(quarter if kind == 0 else -quarter)[0]
        return pltpu.make_async_remote_copy(
            src_ref=passing.at[kind],
            dst_ref=outs.at[(kind, 1 - end_zh) + slot],
            send_sem=o_cross_send.at[kind],
            recv_sem=o_cross_recv.at[kind],
            device_id=legs[kind],
            device_id_type=MESH,
        )

    def swap(kind):
        return pltpu.make_async_remote_copy(
            src_ref=staged.at[kind],
            dst_ref=outs.at[(kind, place.zh) + new_slot],
            send_sem=swap_send.at[kind],
            recv_sem=swap_recv.at[kind],
            device_id=swap_device,
            device_id_type=MESH,
        )

    def direct(kind):
        return pltpu.make_async_remote_copy(
            src_ref=staged.at[kind],
            dst_ref=outs.at[(kind, place.zh) + new_slot],
            send_sem=o_cross_send.at[kind],
            recv_sem=o_cross_recv.at[kind],
            device_id=swap_across,
            device_id_type=MESH,
        )

    @pl.when(stays)
    def _():
        for kind in (0, 1):
            leg(kind).start()
        for kind in (0, 1):
            outs[(kind, place.zh) + slot] = staged[kind]

    @pl.when(moves)
    def _():
        for kind in (0, 1):
            swap(kind).start()
        for kind in (0, 1):
            direct(kind).start()
        for kind in (0, 1):
            swap(kind).wait_recv()

    spread = Gather(place, outs, o_ring_send, o_ring_recv, o_pair_send, o_pair_recv)
    spread.start(0)
    gather.finish(0)

    @pl.when(stays)
    def _():
        for kind in (0, 1):
            leg(kind).wait_recv()
            second_leg(kind).start()

    block = shares.shape[-1]

    def share(target, source):
        return pltpu.make_async_remote_copy(
            src_ref=shares.at[target],
            dst_ref=arrived.at[source],
            send_sem=share_send.at[target],
            recv_sem=share_recv.at[source],
            device_id=(me, target),
            device_id_type=MESH,
        )

    def send_shares(zh):
        total = jnp.zeros((NX * block, w_out.shape[1]), jnp.float32)
        for kind in (0, 1):
            for plane in (0, 1):
                tokens = outs[kind, zh, :, :, plane].reshape(NX * block, half)
                total = total + last_dims(tokens, w_out[plane, :, kind * half : (kind + 1) * half])
        for x in range(NX):
            target = zh * NX + x
            shares[target] = total[x * block : (x + 1) * block].T.astype(jnp.bfloat16)

            @pl.when(target != place.head)
            def _():
                share(target, place.head).start()

    spread.spread(0)
    gather.finish(1)
    spread.hand_on(0)
    for kind in (0, 1):
        direct(kind).wait_recv()
    spread.start(1)
    spread.complete(0)
    spread.spread(1)
    loads[8].wait()
    w_copy.wait_recv()
    spread.from_sibling(0)
    send_shares(place.zh)
    spread.hand_on(1)
    spread.complete(1)
    spread.from_sibling(1)
    send_shares(1 - place.zh)
    spread.finish(0)
    spread.finish(1)

    arrived[place.head] = shares[place.head]
    for source in range(heads):

        @pl.when(source != place.head)
        def _():
            share(source, source).wait_recv()

    total = jnp.zeros(mixed.shape, jnp.float32)
    source_lane = lax.broadcasted_iota(jnp.int32, (block, mixed.shape[1]), 0)
    token = lax.broadcasted_iota(jnp.int32, (block, mixed.shape[1]), 1)
    for plane in (0, 1):
        part = jnp.zeros(shares.shape[1:], jnp.float32)
        for source in range(plane, heads, 2):
            part = part + arrived[source].astype(jnp.float32)
        lane_of = lax.div(token, 2 * rows) * rows + lax.rem(token, rows)
        here = jnp.logical_and(lane_of == source_lane, lax.rem(lax.div(token, rows), 2) == plane)
        total = total + jnp.dot(
            part.astype(jnp.bfloat16), jnp.where(here, 1.0, 0.0).astype(jnp.bfloat16), preferred_element_type=jnp.float32
        )
    mixed[...] = total.astype(jnp.bfloat16)

    w_copy.wait_send()

    @pl.when(is_end)
    def _():
        for j in range(half_heads):
            for kind in (0, 1):
                key_cross(kind, j).wait_send()

    @pl.when(stays)
    def _():
        for kind in (0, 1):
            leg(kind).wait_send()
            second_leg(kind).wait_send()

    @pl.when(moves)
    def _():
        for kind in (0, 1):
            swap(kind).wait_send()
            direct(kind).wait_send()

    for target in range(heads):

        @pl.when(target != place.head)
        def _():
            share(target, place.head).wait_send()


def gather_scratch():
    return [
        pltpu.SemaphoreType.DMA((4 * RING,)),
        pltpu.SemaphoreType.DMA((4 * RING,)),
        pltpu.SemaphoreType.DMA((16,)),
        pltpu.SemaphoreType.DMA((16,)),
    ]


def on_device(
    heads,
    q_nope,
    q_rope,
    prefix_latent,
    prefix_rope,
    group_latent,
    group_rope,
    lengths,
    offset,
    w_uk,
    w_uv,
    w_out,
):
    rows, lat = prefix_latent.shape
    h_dev = w_uk.shape[0]
    q_rows = rows * h_dev
    width = lat + 128
    columns = w_out.shape[1]
    half = h_dev * VD // 2
    frequency = 10000.0 ** (-2.0 * (np.arange(128) % (ROPE // 2)) / ROPE)
    frequency = jnp.asarray(frequency[None, :], jnp.float32)

    tokens = rows * 2 * 2 * NX * NY
    block = rows * NY
    vmem = pl.BlockSpec(memory_space=pltpu.VMEM)
    smem = pl.BlockSpec(memory_space=pltpu.SMEM)
    anywhere = pl.BlockSpec(memory_space=pl.ANY)
    dma = pltpu.SemaphoreType.DMA
    mixed = pl.pallas_call(
        functools.partial(kernel, heads),
        out_shape=jax.ShapeDtypeStruct((columns, tokens // heads), jnp.bfloat16),
        in_specs=[smem] * 2 + [anywhere] * 10,
        out_specs=vmem,
        scratch_shapes=[
            pltpu.VMEM((2, 2, NX, NY, 2, rows, width), jnp.bfloat16),
            pltpu.VMEM((q_rows, width), jnp.bfloat16),
            pltpu.VMEM((q_rows, 1), jnp.float32),
            pltpu.VMEM((q_rows, 1), jnp.float32),
            pltpu.VMEM((q_rows, lat), jnp.float32),
            pltpu.VMEM((2, 2, NX, NY, 2, rows, half), jnp.bfloat16),
            pltpu.VMEM((2, rows, half), jnp.bfloat16),
            pltpu.VMEM((2, rows, half), jnp.bfloat16),
            pltpu.VMEM((2, columns, 2 * half), jnp.bfloat16),
            pltpu.VMEM((heads, columns, block), jnp.bfloat16),
            pltpu.VMEM((heads, columns, block), jnp.bfloat16),
            pltpu.VMEM(q_nope.shape, jnp.bfloat16),
            pltpu.VMEM(q_rope.shape, jnp.bfloat16),
            pltpu.VMEM(prefix_rope.shape, jnp.bfloat16),
            pltpu.VMEM(group_rope.shape, jnp.bfloat16),
            pltpu.VMEM(w_uk.shape, jnp.bfloat16),
            pltpu.VMEM(w_uv.shape, jnp.bfloat16),
            pltpu.VMEM((1, 128), jnp.float32),
            dma((10,)),
        ]
        + gather_scratch()
        + [dma((heads,)), dma((2,))]
        + gather_scratch()
        + [dma((2,)), dma((2,)), dma((2,)), dma((2,)), dma((2,)), dma((2,))]
        + [dma(()), dma(()), dma((heads,)), dma((heads,))],
        compiler_params=pltpu.CompilerParams(
            collective_id=0, has_side_effects=True, vmem_limit_bytes=60 * 1024 * 1024
        ),
        name="attention_and_output",
    )(
        lengths,
        offset,
        q_nope,
        q_rope,
        prefix_latent,
        prefix_rope,
        group_latent,
        group_rope,
        frequency,
        w_uk,
        w_uv,
        w_out.T,
    )
    return mixed.T


def solution(mesh):
    return jax.shard_map(
        functools.partial(on_device, mesh.shape["head"]),
        mesh=mesh,
        in_specs=(
            P("ctx", "head"),
            P("ctx", "head"),
            P("ctx", None),
            P("ctx", None),
            P("ctx", None),
            P("ctx", None),
            P("ctx"),
            P(),
            P("head", None, None),
            P("head", None, None),
            P("head", "ctx"),
        ),
        out_specs=P("head", "ctx"),
        check_vma=False,
    )
```

time: 842 us -> 80.4 us (0.10)
  the two profiles are of different devices: /device:TPU:6 before, /device:TPU:97 now
where the time goes in v1:
time: 80.4 us; the launch traced here: 80.2 us
  Pallas kernels  77.4 us (96%)
  local copies, waits for them, and re-layouts  1.45 us (2%)
  between operations  1.3 us (2%)
    pallas_call x1, Pallas kernels, on_device(): pl.pallas_call(functools.partial(kernel, heads), out_shape=jax.ShapeDtype...  77.4 us

profile of v1, /device:TPU:97, one launch (start us, length us, event | category | flops | bytes accessed | tf_op | source)
XLA Modules:
  0.0 80.2 jit_solution(366438857010267789)
XLA Ops:
  1.3 77.4 %attention_and_output.1 = bf16[112,256]{1,0:T(8,128)(2,1)} custom-call(s32[1]{0:T(128)S(6)} %copy.14.lengths, s32[1]{0:T(128)S(6)} %copy.15.offset, bf16[32,1024]{1,0:T(8,128)(2,1)} %q_nope_any.1, bf16[32,512]{1,0:T(8,128)(2,1)} %q_rope_any.1, bf16[32,512]{1,0:T(8,128)(2,1)} %prefix_latent.1, bf16[32,64]{1,0:T(8,128)(2,1)} %prefix_rope_any.1, ...), custom_call_target="tpu_custom_call" | custom-call | tf_op jit(solution)/shard_map/attention_and_output/pallas_call | solution.py:641
  78.7 1.4 %copy.16 = bf16[256,112]{0,1:T(8,128)(2,1)} copy(bf16[256,112]{0,1:T(8,128)(2,1)} %bitcast.3) | data formatting | bytes 114688

commit v2 on v1

--- a/solution.py
+++ b/solution.py
@@ -15,6 +15,7 @@
 NX = 4
 NY = 4
 HIDDEN = -1e30
+UNUSED = 1024.0
 MESH = pl.DeviceIdType.MESH
 
 
@@ -142,12 +143,14 @@
         for kind in (0, 1):
             self.pair(kind, plane, 0).start()
 
-    def hand_on(self, plane):
-        for o in range(4):
+    def hand_on(self, plane, offsets=(0, 1, 2, 3)):
+        for o in offsets:
             for kind in (0, 1):
                 for direction in (0, 1):
                     self.second(kind, plane, o, direction).wait_recv()
                 self.relay(kind, plane, o).start()
+
+    def hand_over(self, plane):
         for piece in (1, 2):
             for kind in (0, 1):
                 self.pair(kind, plane, piece).start()
@@ -158,9 +161,9 @@
                 self.relay(kind, plane, o).wait_recv()
             self.pair(kind, plane, 3).start()
 
-    def from_sibling(self, plane):
-        for kind in (0, 1):
-            for piece in range(4):
+    def from_sibling(self, plane, pieces=(0, 1, 2, 3)):
+        for kind in (0, 1):
+            for piece in pieces:
                 self.pair(kind, plane, piece).wait_recv()
 
     def finish(self, plane):
@@ -210,7 +213,8 @@
     w_out_any,
     mixed,
     keys,
-    query,
+    prefix_query,
+    group_query,
     row_max,
     row_sum,
     accum,
@@ -252,7 +256,7 @@
     place = Place(heads)
     rows, lat = prefix_latent.shape
     h_dev = w_uk.shape[0]
-    width = keys.shape[-1]
+    part = rows // 2
     half = staged.shape[-1]
     half_heads = heads // 2
     me = place.ctx()
@@ -293,8 +297,8 @@
         pltpu.make_async_copy(src, dst, load_sem.at[i])
         for i, (src, dst) in enumerate(
             (
-                (prefix_latent, keys.at[(0,) + own + (slice(None), pl.ds(0, lat))]),
-                (group_latent, keys.at[(1,) + own + (slice(None), pl.ds(0, lat))]),
+                (prefix_latent.at[pl.ds(0, part)], keys.at[(0,) + own + (slice(None), pl.ds(0, lat))]),
+                (group_latent.at[pl.ds(0, part)], keys.at[(0,) + own + (slice(None), pl.ds(lat + 128, lat))]),
                 (q_nope_any, q_nope),
                 (q_rope_any, q_rope),
                 (prefix_rope_any, prefix_rope),
@@ -303,6 +307,8 @@
                 (w_uv_any, w_uv),
                 (w_out_any, w_out.at[odd]),
                 (frequency_any, frequency),
+                (prefix_latent.at[pl.ds(part, part)], keys.at[(1,) + own + (slice(None), pl.ds(0, lat))]),
+                (group_latent.at[pl.ds(part, part)], keys.at[(1,) + own + (slice(None), pl.ds(lat + 128, lat))]),
             )
         )
     ]
@@ -325,12 +331,13 @@
         value = ref[...].astype(jnp.float32)
         return jnp.concatenate([value, value], axis=1)
 
-    flags = jnp.where(jnp.logical_and(lane == ROPE, row >= lengths[0]), HIDDEN, 0.0)
-    tail = pl.ds(lat, width - lat)
-    keys[(0,) + own + (slice(None), tail)] = jnp.where(lane < ROPE, twice(prefix_rope), flags).astype(jnp.bfloat16)
-    keys[(1,) + own + (slice(None), tail)] = jnp.where(lane < ROPE, turn(twice(group_rope)), 0.0).astype(jnp.bfloat16)
-    loads[0].wait()
-    loads[1].wait()
+    unused = jnp.where(lane == 0, UNUSED, 0.0)
+    ropes = jnp.where(row < lengths[0], twice(prefix_rope), unused)
+    ropes = jnp.where(lane < ROPE, ropes, turn(twice(group_rope))).astype(jnp.bfloat16)
+    for kind in (0, 1):
+        keys[(kind,) + own + (slice(None), pl.ds(lat, 128))] = ropes[kind * part : (kind + 1) * part]
+    for i in (0, 1, 10, 11):
+        loads[i].wait()
 
     pl.semaphore_wait(pltpu.get_barrier_semaphore(), len(peers) + 2 + half_heads * is_end.astype(jnp.int32))
 
@@ -355,49 +362,72 @@
 
     gather.start(0)
 
+    q_rows = h_dev * rows
     loads[2].wait()
     loads[3].wait()
     loads[6].wait()
-    one = jnp.where(lane == ROPE, 1.0, 0.0)
+    mark = jnp.logical_and(lane[:16] == 0, row[:16] == 0)
+    prefix_query[pl.ds(q_rows, 16), pl.ds(0, lat)] = jnp.zeros((16, lat), jnp.bfloat16)
+    prefix_query[pl.ds(q_rows, 16), pl.ds(lat, 128)] = jnp.where(mark, 1.0, 0.0).astype(jnp.bfloat16)
     for pair in range(h_dev // 2):
-        tile = q_rope[:, pair * 128 : (pair + 1) * 128].astype(jnp.float32)
-        turned = turn(tile)
+        turned = turn(q_rope[:, pair * 128 : (pair + 1) * 128].astype(jnp.float32))
+        other = pltpu.roll(turned, ROPE, 1)
         for side in (0, 1):
             head = 2 * pair + side
-            if side == 1:
-                turned = pltpu.roll(turned, ROPE, 1)
-            query[pl.ds(head * rows, rows), pl.ds(lat, width - lat)] = jnp.where(lane < ROPE, turned, one).astype(
-                jnp.bfloat16
-            )
-            query[pl.ds(head * rows, rows), pl.ds(0, lat)] = jnp.dot(
+            at = pl.ds(head * rows, rows)
+            low_part, high_part = (turned, other) if side == 0 else (other, turned)
+            prefix_query[at, pl.ds(lat, 128)] = jnp.where(lane < ROPE, low_part, 0.0).astype(jnp.bfloat16)
+            group_query[at, pl.ds(0, 128)] = jnp.where(lane >= ROPE, high_part, 0.0).astype(jnp.bfloat16)
+            latent = jnp.dot(
                 q_nope[:, head * NOPE : (head + 1) * NOPE], w_uk[head], preferred_element_type=jnp.float32
             ).astype(jnp.bfloat16)
+            prefix_query[at, pl.ds(0, lat)] = latent
+            group_query[at, pl.ds(128, lat)] = latent
 
     row_max[...] = jnp.full(row_max.shape, HIDDEN, jnp.float32)
     row_sum[...] = jnp.zeros(row_sum.shape, jnp.float32)
     accum[...] = jnp.zeros(accum.shape, jnp.float32)
     scale = (NOPE + ROPE) ** -0.5 * math.log2(math.e)
-    q_rows = h_dev * rows
-    chunk = NX * NY * rows
     my_token = me * rows + lax.rem(lax.broadcasted_iota(jnp.int32, (q_rows, 1), 0), rows)
 
-    def attend(kind, zh, core):
-        part = keys[kind, zh, :, :, core].reshape(chunk, width)
-        scores = last_dims(query[...], part) * scale
-        if kind == 1:
-            index = lax.broadcasted_iota(jnp.int32, (1, chunk), 1)
-            place_of = (zh * NX * NY + lax.div(index, rows)) * 2 + core
-            key_token = place_of * rows + lax.rem(index, rows)
-            scores = jnp.where(key_token <= my_token, scores, HIDDEN)
+    def attend(plane, lines):
+        zh = gather.zh(plane)
+        span = NY * part
+        index = lax.broadcasted_iota(jnp.int32, (1, span * len(lines)), 1)
+        inside = lax.rem(index, span)
+        key_token = jnp.zeros(index.shape, jnp.int32)
+        blocks = []
+        for i, (kind, step, sibling) in enumerate(lines):
+            core = 1 - place.core if sibling else place.core
+            if kind == 0:
+                x = lax.rem(place.x + step + NX, NX)
+                blocks.append(keys[0, zh, x, :, core])
+                first, stride = place.ctx(zh=zh, x=x, y=0, core=core), 2
+            else:
+                y = lax.rem(place.y + step + NY, NY)
+                blocks.append(keys[1, zh, :, y, core])
+                first, stride = place.ctx(zh=zh, x=0, y=y, core=core), 2 * NY
+            token = (first + stride * lax.div(inside, part)) * rows + kind * part + lax.rem(inside, part)
+            key_token = jnp.where(lax.div(index, span) == i, token, key_token)
+        rows_in = jnp.concatenate([block.reshape(span, block.shape[-1]) for block in blocks], axis=0)
+        prefix_all = last_dims(prefix_query[...], rows_in[:, : lat + 128])
+        hidden = prefix_all[q_rows : q_rows + 1] > UNUSED / 2
+        prefix_scores = jnp.where(hidden, HIDDEN, prefix_all[:q_rows] * scale)
+        group_scores = last_dims(group_query[...], rows_in[:, lat:]) * scale
+        group_scores = jnp.where(key_token <= my_token, group_scores, HIDDEN)
         old_max = row_max[...]
-        new_max = jnp.maximum(old_max, jnp.max(scores, axis=1, keepdims=True))
-        weights = jnp.exp2(scores - new_max)
+        new_max = jnp.max(jnp.maximum(prefix_scores, group_scores), axis=1, keepdims=True)
+        new_max = jnp.maximum(old_max, new_max)
+        prefix_weights = jnp.exp2(prefix_scores - new_max)
+        group_weights = jnp.exp2(group_scores - new_max)
         factor = jnp.exp2(old_max - new_max)
         row_max[...] = new_max
-        row_sum[...] = row_sum[...] * factor + jnp.sum(weights, axis=1, keepdims=True)
-        accum[...] = accum[...] * factor + jnp.dot(
-            weights.astype(jnp.bfloat16), part[:, :lat], preferred_element_type=jnp.float32
-        )
+        row_sum[...] = row_sum[...] * factor + jnp.sum(prefix_weights + group_weights, axis=1, keepdims=True)
+        taken = jnp.dot(prefix_weights.astype(jnp.bfloat16), rows_in[:, :lat], preferred_element_type=jnp.float32)
+        taken = taken + jnp.dot(
+            group_weights.astype(jnp.bfloat16), rows_in[:, lat + 128 :], preferred_element_type=jnp.float32
+        )
+        accum[...] = accum[...] * factor + taken
 
     w_copy = pltpu.make_async_remote_copy(
         src_ref=w_out_any,
@@ -408,26 +438,34 @@
         device_id_type=MESH,
     )
 
+    def whole(kind, sibling):
+        return [(kind, step, sibling) for step in OFFSETS]
+
+    near = OFFSETS[:3]
     gather.spread(0)
     gather.hand_on(0)
+    gather.hand_over(0)
     for kind in (0, 1):
         key_cross(kind, 0).wait_recv()
     gather.start(1)
     w_copy.start()
     gather.complete(0)
+    attend(0, whole(0, False))
     gather.spread(1)
-    attend(0, place.zh, place.core)
-    gather.hand_on(1)
-    attend(1, place.zh, place.core)
+    attend(0, whole(1, False))
+    gather.hand_on(1, (0,))
     gather.from_sibling(0)
-    attend(0, place.zh, 1 - place.core)
+    attend(0, whole(0, True))
+    gather.hand_on(1, (1, 2))
+    attend(0, whole(1, True))
+    gather.hand_on(1, (3,))
+    gather.hand_over(1)
+    attend(1, [(kind, step, False) for kind in (0, 1) for step in near])
     gather.complete(1)
-    attend(1, place.zh, 1 - place.core)
-    attend(0, 1 - place.zh, place.core)
-    attend(1, 1 - place.zh, place.core)
-    gather.from_sibling(1)
-    attend(0, 1 - place.zh, 1 - place.core)
-    attend(1, 1 - place.zh, 1 - place.core)
+    gather.from_sibling(1, (0, 1, 2))
+    attend(1, [(kind, step, True) for kind in (0, 1) for step in near])
+    gather.from_sibling(1, (3,))
+    attend(1, [(kind, 2, sibling) for kind in (0, 1) for sibling in (False, True)])
 
     loads[7].wait()
     latent_out = (accum[...] / row_sum[...]).astype(jnp.bfloat16)
@@ -519,12 +557,18 @@
             device_id_type=MESH,
         )
 
-    def send_shares(zh):
+    def part_share(zh, plane):
         total = jnp.zeros((NX * block, w_out.shape[1]), jnp.float32)
         for kind in (0, 1):
-            for plane in (0, 1):
-                tokens = outs[kind, zh, :, :, plane].reshape(NX * block, half)
-                total = total + last_dims(tokens, w_out[plane, :, kind * half : (kind + 1) * half])
+            tokens = outs[kind, zh, :, :, plane].reshape(NX * block, half)
+            total = total + last_dims(tokens, w_out[plane, :, kind * half : (kind + 1) * half])
+        return total
+
+    def send_shares(plane):
+        zh = spread.zh(plane)
+        total = part_share(zh, place.core)
+        spread.from_sibling(plane)
+        total = total + part_share(zh, 1 - place.core)
         for x in range(NX):
             target = zh * NX + x
             shares[target] = total[x * block : (x + 1) * block].T.astype(jnp.bfloat16)
@@ -536,6 +580,7 @@
     spread.spread(0)
     gather.finish(1)
     spread.hand_on(0)
+    spread.hand_over(0)
     for kind in (0, 1):
         direct(kind).wait_recv()
     spread.start(1)
@@ -543,12 +588,11 @@
     spread.spread(1)
     loads[8].wait()
     w_copy.wait_recv()
-    spread.from_sibling(0)
-    send_shares(place.zh)
+    send_shares(0)
     spread.hand_on(1)
+    spread.hand_over(1)
     spread.complete(1)
-    spread.from_sibling(1)
-    send_shares(1 - place.zh)
+    send_shares(1)
     spread.finish(0)
     spread.finish(1)
 
@@ -626,7 +670,7 @@
     rows, lat = prefix_latent.shape
     h_dev = w_uk.shape[0]
     q_rows = rows * h_dev
-    width = lat + 128
+    width = 2 * lat + 128
     columns = w_out.shape[1]
     half = h_dev * VD // 2
     frequency = 10000.0 ** (-2.0 * (np.arange(128) % (ROPE // 2)) / ROPE)
@@ -644,8 +688,9 @@
         in_specs=[smem] * 2 + [anywhere] * 10,
         out_specs=vmem,
         scratch_shapes=[
-            pltpu.VMEM((2, 2, NX, NY, 2, rows, width), jnp.bfloat16),
-            pltpu.VMEM((q_rows, width), jnp.bfloat16),
+            pltpu.VMEM((2, 2, NX, NY, 2, rows // 2, width), jnp.bfloat16),
+            pltpu.VMEM((q_rows + 16, lat + 128), jnp.bfloat16),
+            pltpu.VMEM((q_rows, lat + 128), jnp.bfloat16),
             pltpu.VMEM((q_rows, 1), jnp.float32),
             pltpu.VMEM((q_rows, 1), jnp.float32),
             pltpu.VMEM((q_rows, lat), jnp.float32),
@@ -662,7 +707,7 @@
             pltpu.VMEM(w_uk.shape, jnp.bfloat16),
             pltpu.VMEM(w_uv.shape, jnp.bfloat16),
             pltpu.VMEM((1, 128), jnp.float32),
-            dma((10,)),
+            dma((12,)),
         ]
         + gather_scratch()
         + [dma((heads,)), dma((2,))]

time: 80.4 us -> 80.1 us (level)
  no operation moved by 1% of the time
where the time goes in v2:
time: 80.1 us; the launch traced here: 79.9 us
  Pallas kernels  77.1 us (96%)
  local copies, waits for them, and re-layouts  1.45 us (2%)
  between operations  1.3 us (2%)
    pallas_call x1, Pallas kernels, on_device(): pl.pallas_call(functools.partial(kernel, heads), out_shape=jax.ShapeDtype...  77.1 us

profile of v2, /device:TPU:97, one launch (start us, length us, event | category | flops | bytes accessed | tf_op | source)
XLA Modules:
  0.0 79.9 jit_solution(14731578044119633603)
XLA Ops:
  1.3 77.1 %attention_and_output.1 = bf16[112,256]{1,0:T(8,128)(2,1)} custom-call(s32[1]{0:T(128)S(6)} %copy.14.lengths, s32[1]{0:T(128)S(6)} %copy.15.offset, bf16[32,1024]{1,0:T(8,128)(2,1)} %q_nope_any.1, bf16[32,512]{1,0:T(8,128)(2,1)} %q_rope_any.1, bf16[32,512]{1,0:T(8,128)(2,1)} %prefix_latent.1, bf16[32,64]{1,0:T(8,128)(2,1)} %prefix_rope_any.1, ...), custom_call_target="tpu_custom_call" | custom-call | tf_op jit(solution)/shard_map/attention_and_output/pallas_call | solution.py:685
  78.4 1.4 %copy.16 = bf16[256,112]{0,1:T(8,128)(2,1)} copy(bf16[256,112]{0,1:T(8,128)(2,1)} %bitcast.3) | data formatting | bytes 114688

commit v3 on v2

--- a/solution.py
+++ b/solution.py
@@ -224,6 +224,7 @@
     w_out,
     shares,
     arrived,
+    passed,
     q_nope,
     q_rope,
     prefix_rope,
@@ -252,6 +253,8 @@
     w_recv,
     share_send,
     share_recv,
+    hop_send,
+    hop_recv,
 ):
     place = Place(heads)
     rows, lat = prefix_latent.shape
@@ -362,6 +365,8 @@
 
     gather.start(0)
 
+    scale = (NOPE + ROPE) ** -0.5 * math.log2(math.e)
+
     q_rows = h_dev * rows
     loads[2].wait()
     loads[3].wait()
@@ -370,7 +375,7 @@
     prefix_query[pl.ds(q_rows, 16), pl.ds(0, lat)] = jnp.zeros((16, lat), jnp.bfloat16)
     prefix_query[pl.ds(q_rows, 16), pl.ds(lat, 128)] = jnp.where(mark, 1.0, 0.0).astype(jnp.bfloat16)
     for pair in range(h_dev // 2):
-        turned = turn(q_rope[:, pair * 128 : (pair + 1) * 128].astype(jnp.float32))
+        turned = turn(q_rope[:, pair * 128 : (pair + 1) * 128].astype(jnp.float32)) * scale
         other = pltpu.roll(turned, ROPE, 1)
         for side in (0, 1):
             head = 2 * pair + side
@@ -380,14 +385,14 @@
             group_query[at, pl.ds(0, 128)] = jnp.where(lane >= ROPE, high_part, 0.0).astype(jnp.bfloat16)
             latent = jnp.dot(
                 q_nope[:, head * NOPE : (head + 1) * NOPE], w_uk[head], preferred_element_type=jnp.float32
-            ).astype(jnp.bfloat16)
+            )
+            latent = (latent * scale).astype(jnp.bfloat16)
             prefix_query[at, pl.ds(0, lat)] = latent
             group_query[at, pl.ds(128, lat)] = latent
 
     row_max[...] = jnp.full(row_max.shape, HIDDEN, jnp.float32)
     row_sum[...] = jnp.zeros(row_sum.shape, jnp.float32)
     accum[...] = jnp.zeros(accum.shape, jnp.float32)
-    scale = (NOPE + ROPE) ** -0.5 * math.log2(math.e)
     my_token = me * rows + lax.rem(lax.broadcasted_iota(jnp.int32, (q_rows, 1), 0), rows)
 
     def attend(plane, lines):
@@ -412,8 +417,8 @@
         rows_in = jnp.concatenate([block.reshape(span, block.shape[-1]) for block in blocks], axis=0)
         prefix_all = last_dims(prefix_query[...], rows_in[:, : lat + 128])
         hidden = prefix_all[q_rows : q_rows + 1] > UNUSED / 2
-        prefix_scores = jnp.where(hidden, HIDDEN, prefix_all[:q_rows] * scale)
-        group_scores = last_dims(group_query[...], rows_in[:, lat:]) * scale
+        prefix_scores = jnp.where(hidden, HIDDEN, prefix_all[:q_rows])
+        group_scores = last_dims(group_query[...], rows_in[:, lat:])
         group_scores = jnp.where(key_token <= my_token, group_scores, HIDDEN)
         old_max = row_max[...]
         new_max = jnp.max(jnp.maximum(prefix_scores, group_scores), axis=1, keepdims=True)
@@ -422,7 +427,11 @@
         group_weights = jnp.exp2(group_scores - new_max)
         factor = jnp.exp2(old_max - new_max)
         row_max[...] = new_max
-        row_sum[...] = row_sum[...] * factor + jnp.sum(prefix_weights + group_weights, axis=1, keepdims=True)
+        weights = prefix_weights + group_weights
+        lanes = weights[:, :128]
+        for j in range(1, weights.shape[1] // 128):
+            lanes = lanes + weights[:, j * 128 : (j + 1) * 128]
+        row_sum[...] = row_sum[...] * factor + lanes
         taken = jnp.dot(prefix_weights.astype(jnp.bfloat16), rows_in[:, :lat], preferred_element_type=jnp.float32)
         taken = taken + jnp.dot(
             group_weights.astype(jnp.bfloat16), rows_in[:, lat + 128 :], preferred_element_type=jnp.float32
@@ -438,37 +447,38 @@
         device_id_type=MESH,
     )
 
-    def whole(kind, sibling):
-        return [(kind, step, sibling) for step in OFFSETS]
-
-    near = OFFSETS[:3]
+    def pick(steps, sibling):
+        return [(kind, step, sibling) for kind in (0, 1) for step in steps]
+
     gather.spread(0)
+    attend(0, pick((0,), False))
     gather.hand_on(0)
     gather.hand_over(0)
     for kind in (0, 1):
         key_cross(kind, 0).wait_recv()
     gather.start(1)
     w_copy.start()
+    attend(0, pick((-1, 1), False))
     gather.complete(0)
-    attend(0, whole(0, False))
     gather.spread(1)
-    attend(0, whole(1, False))
+    gather.from_sibling(0, (0, 1, 2))
+    attend(0, pick((0, -1), True))
     gather.hand_on(1, (0,))
-    gather.from_sibling(0)
-    attend(0, whole(0, True))
+    attend(0, [(kind, 2, False) for kind in (0, 1)] + [(kind, 1, True) for kind in (0, 1)])
     gather.hand_on(1, (1, 2))
-    attend(0, whole(1, True))
     gather.hand_on(1, (3,))
     gather.hand_over(1)
-    attend(1, [(kind, step, False) for kind in (0, 1) for step in near])
+    attend(1, pick((0, -1, 1), False))
     gather.complete(1)
+    gather.from_sibling(0, (3,))
     gather.from_sibling(1, (0, 1, 2))
-    attend(1, [(kind, step, True) for kind in (0, 1) for step in near])
+    attend(1, pick((0, -1, 1), True))
+    attend(0, pick((2,), True))
     gather.from_sibling(1, (3,))
-    attend(1, [(kind, 2, sibling) for kind in (0, 1) for sibling in (False, True)])
+    attend(1, pick((2,), False) + pick((2,), True))
 
     loads[7].wait()
-    latent_out = (accum[...] / row_sum[...]).astype(jnp.bfloat16)
+    latent_out = (accum[...] / jnp.sum(row_sum[...], axis=1, keepdims=True)).astype(jnp.bfloat16)
     per_kind = half // VD
     for head in range(h_dev):
         staged[head // per_kind, :, pl.ds((head % per_kind) * VD, VD)] = jnp.dot(
@@ -547,13 +557,34 @@
 
     block = shares.shape[-1]
 
-    def share(target, source):
+    quad = heads // 2
+    my_quad = lax.div(place.head, quad)
+    inner = jnp.logical_and(place.head >= quad // 2, place.head < quad + quad // 2)
+    outer = jnp.logical_not(inner)
+
+    def share(target, slot):
         return pltpu.make_async_remote_copy(
             src_ref=shares.at[target],
-            dst_ref=arrived.at[source],
+            dst_ref=arrived.at[slot],
             send_sem=share_send.at[target],
-            recv_sem=share_recv.at[source],
+            recv_sem=share_recv.at[slot],
             device_id=(me, target),
+            device_id_type=MESH,
+        )
+
+    def near_share(target):
+        return share(target, lax.rem(place.head, quad))
+
+    def far_share(target):
+        return share(target, quad + lax.rem(place.head, 2))
+
+    def hop(target, x):
+        return pltpu.make_async_remote_copy(
+            src_ref=shares.at[target],
+            dst_ref=passed.at[x],
+            send_sem=hop_send.at[x],
+            recv_sem=hop_recv.at[x],
+            device_id=(me, jnp.where(place.head < quad, place.head + 2, place.head - 2)),
             device_id_type=MESH,
         )
 
@@ -573,9 +604,25 @@
             target = zh * NX + x
             shares[target] = total[x * block : (x + 1) * block].T.astype(jnp.bfloat16)
 
-            @pl.when(target != place.head)
+            @pl.when(jnp.logical_and(my_quad == zh, target != place.head))
             def _():
-                share(target, place.head).start()
+                near_share(target).start()
+
+            @pl.when(jnp.logical_and(my_quad != zh, outer))
+            def _():
+                hop(target, x).start()
+
+    def forward_shares(plane):
+        zh = spread.zh(plane)
+
+        @pl.when(jnp.logical_and(my_quad != zh, inner))
+        def _():
+            for x in range(NX):
+                target = zh * NX + x
+                hop(target, x).wait_recv()
+                total = shares[target].astype(jnp.float32) + passed[x].astype(jnp.float32)
+                shares[target] = total.astype(jnp.bfloat16)
+                far_share(target).start()
 
     spread.spread(0)
     gather.finish(1)
@@ -589,31 +636,38 @@
     loads[8].wait()
     w_copy.wait_recv()
     send_shares(0)
-    spread.hand_on(1)
+    spread.hand_on(1, (0, 1))
+    spread.hand_on(1, (2, 3))
     spread.hand_over(1)
+    forward_shares(0)
     spread.complete(1)
     send_shares(1)
+    forward_shares(1)
     spread.finish(0)
     spread.finish(1)
 
-    arrived[place.head] = shares[place.head]
-    for source in range(heads):
-
-        @pl.when(source != place.head)
+    own_slot = lax.rem(place.head, quad)
+    arrived[own_slot] = shares[place.head]
+    for source in range(quad):
+
+        @pl.when(source != own_slot)
         def _():
-            share(source, source).wait_recv()
+            share(place.head, source).wait_recv()
+
+    for source in (quad, quad + 1):
+        share(place.head, source).wait_recv()
 
     total = jnp.zeros(mixed.shape, jnp.float32)
     source_lane = lax.broadcasted_iota(jnp.int32, (block, mixed.shape[1]), 0)
     token = lax.broadcasted_iota(jnp.int32, (block, mixed.shape[1]), 1)
     for plane in (0, 1):
-        part = jnp.zeros(shares.shape[1:], jnp.float32)
-        for source in range(plane, heads, 2):
-            part = part + arrived[source].astype(jnp.float32)
+        summed = jnp.zeros(shares.shape[1:], jnp.float32)
+        for source in range(plane, quad + 2, 2):
+            summed = summed + arrived[source].astype(jnp.float32)
         lane_of = lax.div(token, 2 * rows) * rows + lax.rem(token, rows)
         here = jnp.logical_and(lane_of == source_lane, lax.rem(lax.div(token, rows), 2) == plane)
         total = total + jnp.dot(
-            part.astype(jnp.bfloat16), jnp.where(here, 1.0, 0.0).astype(jnp.bfloat16), preferred_element_type=jnp.float32
+            summed.astype(jnp.bfloat16), jnp.where(here, 1.0, 0.0).astype(jnp.bfloat16), preferred_element_type=jnp.float32
         )
     mixed[...] = total.astype(jnp.bfloat16)
 
@@ -637,11 +691,19 @@
             swap(kind).wait_send()
             direct(kind).wait_send()
 
-    for target in range(heads):
-
-        @pl.when(target != place.head)
+    for x in range(NX):
+
+        @pl.when(x != own_slot)
         def _():
-            share(target, place.head).wait_send()
+            near_share(my_quad * quad + x).wait_send()
+
+        @pl.when(inner)
+        def _():
+            far_share((1 - my_quad) * quad + x).wait_send()
+
+        @pl.when(outer)
+        def _():
+            hop((1 - my_quad) * quad + x, x).wait_send()
 
 
 def gather_scratch():
@@ -684,7 +746,7 @@
     dma = pltpu.SemaphoreType.DMA
     mixed = pl.pallas_call(
         functools.partial(kernel, heads),
-        out_shape=jax.ShapeDtypeStruct((columns, tokens // heads), jnp.bfloat16),
+        out_shape=pltpu.VMEM((columns, tokens // heads), jnp.bfloat16),
         in_specs=[smem] * 2 + [anywhere] * 10,
         out_specs=vmem,
         scratch_shapes=[
@@ -692,14 +754,15 @@
             pltpu.VMEM((q_rows + 16, lat + 128), jnp.bfloat16),
             pltpu.VMEM((q_rows, lat + 128), jnp.bfloat16),
             pltpu.VMEM((q_rows, 1), jnp.float32),
-            pltpu.VMEM((q_rows, 1), jnp.float32),
+            pltpu.VMEM((q_rows, 128), jnp.float32),
             pltpu.VMEM((q_rows, lat), jnp.float32),
             pltpu.VMEM((2, 2, NX, NY, 2, rows, half), jnp.bfloat16),
             pltpu.VMEM((2, rows, half), jnp.bfloat16),
             pltpu.VMEM((2, rows, half), jnp.bfloat16),
             pltpu.VMEM((2, columns, 2 * half), jnp.bfloat16),
             pltpu.VMEM((heads, columns, block), jnp.bfloat16),
-            pltpu.VMEM((heads, columns, block), jnp.bfloat16),
+            pltpu.VMEM((heads // 2 + 2, columns, block), jnp.bfloat16),
+            pltpu.VMEM((NX, columns, block), jnp.bfloat16),
             pltpu.VMEM(q_nope.shape, jnp.bfloat16),
             pltpu.VMEM(q_rope.shape, jnp.bfloat16),
             pltpu.VMEM(prefix_rope.shape, jnp.bfloat16),
@@ -713,7 +776,7 @@
         + [dma((heads,)), dma((2,))]
         + gather_scratch()
         + [dma((2,)), dma((2,)), dma((2,)), dma((2,)), dma((2,)), dma((2,))]
-        + [dma(()), dma(()), dma((heads,)), dma((heads,))],
+        + [dma(()), dma(()), dma((heads,)), dma((heads // 2 + 2,)), dma((NX,)), dma((NX,))],
         compiler_params=pltpu.CompilerParams(
             collective_id=0, has_side_effects=True, vmem_limit_bytes=60 * 1024 * 1024
         ),

time: 80.1 us -> 76.1 us (0.950)
  the two profiles are of different devices: /device:TPU:97 before, /device:TPU:64 now
where the time goes in v3:
time: 76.1 us; the launch traced here: 75.9 us
  Pallas kernels  74 us (97%)
  between operations  1.3 us (2%)
    pallas_call x1, Pallas kernels, on_device(): pl.pallas_call(functools.partial(kernel, heads), out_shape=pltpu.VMEM((co...  74 us

profile of v3, /device:TPU:64, one launch (start us, length us, event | category | flops | bytes accessed | tf_op | source)
XLA Modules:
  0.0 75.9 jit_solution(2506667907712219568)
XLA Ops:
  1.3 74.0 %attention_and_output.1 = bf16[112,256]{1,0:T(8,128)(2,1)S(1)} custom-call(s32[1]{0:T(128)S(6)} %copy.15.lengths, s32[1]{0:T(128)S(6)} %copy.16.offset, bf16[32,1024]{1,0:T(8,128)(2,1)} %q_nope_any.1, bf16[32,512]{1,0:T(8,128)(2,1)} %q_rope_any.1, bf16[32,512]{1,0:T(8,128)(2,1)} %prefix_latent.1, bf16[32,64]{1,0:T(8,128)(2,1)} %prefix_rope_any.1, ...), custom_call_target="tpu_custom_call" | custom-call | tf_op jit(solution)/shard_map/attention_and_output/pallas_call | solution.py:747
  75.3 0.6 copy.14

commit v4 on v3

--- a/solution.py
+++ b/solution.py
@@ -420,23 +420,19 @@
         prefix_scores = jnp.where(hidden, HIDDEN, prefix_all[:q_rows])
         group_scores = last_dims(group_query[...], rows_in[:, lat:])
         group_scores = jnp.where(key_token <= my_token, group_scores, HIDDEN)
-        old_max = row_max[...]
-        new_max = jnp.max(jnp.maximum(prefix_scores, group_scores), axis=1, keepdims=True)
-        new_max = jnp.maximum(old_max, new_max)
-        prefix_weights = jnp.exp2(prefix_scores - new_max)
-        group_weights = jnp.exp2(group_scores - new_max)
-        factor = jnp.exp2(old_max - new_max)
-        row_max[...] = new_max
-        weights = prefix_weights + group_weights
-        lanes = weights[:, :128]
-        for j in range(1, weights.shape[1] // 128):
-            lanes = lanes + weights[:, j * 128 : (j + 1) * 128]
-        row_sum[...] = row_sum[...] * factor + lanes
-        taken = jnp.dot(prefix_weights.astype(jnp.bfloat16), rows_in[:, :lat], preferred_element_type=jnp.float32)
-        taken = taken + jnp.dot(
-            group_weights.astype(jnp.bfloat16), rows_in[:, lat + 128 :], preferred_element_type=jnp.float32
-        )
-        accum[...] = accum[...] * factor + taken
+        for scores, values in ((prefix_scores, rows_in[:, :lat]), (group_scores, rows_in[:, lat + 128 :])):
+            old_max = row_max[...]
+            new_max = jnp.maximum(old_max, jnp.max(scores, axis=1, keepdims=True))
+            weights = jnp.exp2(scores - new_max)
+            factor = jnp.exp2(old_max - new_max)
+            row_max[...] = new_max
+            lanes = weights[:, :128]
+            for j in range(1, weights.shape[1] // 128):
+                lanes = lanes + weights[:, j * 128 : (j + 1) * 128]
+            row_sum[...] = row_sum[...] * factor + lanes
+            accum[...] = accum[...] * factor + jnp.dot(
+                weights.astype(jnp.bfloat16), values, preferred_element_type=jnp.float32
+            )
 
     w_copy = pltpu.make_async_remote_copy(
         src_ref=w_out_any,
@@ -454,36 +450,38 @@
     attend(0, pick((0,), False))
     gather.hand_on(0)
     gather.hand_over(0)
+    gather.from_sibling(0, (0,))
+    attend(0, pick((0,), True))
     for kind in (0, 1):
         key_cross(kind, 0).wait_recv()
     gather.start(1)
     w_copy.start()
+    gather.complete(0)
     attend(0, pick((-1, 1), False))
-    gather.complete(0)
     gather.spread(1)
-    gather.from_sibling(0, (0, 1, 2))
-    attend(0, pick((0, -1), True))
-    gather.hand_on(1, (0,))
-    attend(0, [(kind, 2, False) for kind in (0, 1)] + [(kind, 1, True) for kind in (0, 1)])
-    gather.hand_on(1, (1, 2))
-    gather.hand_on(1, (3,))
+    gather.from_sibling(0, (1, 2))
+    attend(0, pick((-1, 1), True))
+    gather.hand_on(1, (0, 1))
+    gather.from_sibling(0, (3,))
+    attend(0, pick((2,), False) + pick((2,), True))
+    gather.hand_on(1, (2, 3))
     gather.hand_over(1)
     attend(1, pick((0, -1, 1), False))
     gather.complete(1)
-    gather.from_sibling(0, (3,))
     gather.from_sibling(1, (0, 1, 2))
     attend(1, pick((0, -1, 1), True))
-    attend(0, pick((2,), True))
     gather.from_sibling(1, (3,))
     attend(1, pick((2,), False) + pick((2,), True))
 
     loads[7].wait()
     latent_out = (accum[...] / jnp.sum(row_sum[...], axis=1, keepdims=True)).astype(jnp.bfloat16)
     per_kind = half // VD
-    for head in range(h_dev):
-        staged[head // per_kind, :, pl.ds((head % per_kind) * VD, VD)] = jnp.dot(
-            latent_out[head * rows : (head + 1) * rows], w_uv[head], preferred_element_type=jnp.float32
-        ).astype(jnp.bfloat16)
+
+    def head_outputs(kind):
+        for head in range(kind * per_kind, (kind + 1) * per_kind):
+            staged[kind, :, pl.ds((head % per_kind) * VD, VD)] = jnp.dot(
+                latent_out[head * rows : (head + 1) * rows], w_uv[head], preferred_element_type=jnp.float32
+            ).astype(jnp.bfloat16)
 
     slot = (place.x, place.y, place.core)
     new_slot = (place.x, place.y, 1 - place.core)
@@ -529,19 +527,21 @@
             device_id_type=MESH,
         )
 
-    @pl.when(stays)
-    def _():
-        for kind in (0, 1):
+    for kind in (0, 1):
+        head_outputs(kind)
+
+        @pl.when(stays)
+        def _():
             leg(kind).start()
-        for kind in (0, 1):
             outs[(kind, place.zh) + slot] = staged[kind]
+
+        @pl.when(moves)
+        def _():
+            swap(kind).start()
+            direct(kind).start()
 
     @pl.when(moves)
     def _():
-        for kind in (0, 1):
-            swap(kind).start()
-        for kind in (0, 1):
-            direct(kind).start()
         for kind in (0, 1):
             swap(kind).wait_recv()
 

time: 76.1 us -> 77.7 us (1.021)
  the two profiles are of different devices: /device:TPU:64 before, /device:TPU:102 now
where the time goes in v4:
time: 77.7 us; the launch traced here: 77.5 us
  Pallas kernels  75.6 us (97%)
  between operations  1.3 us (2%)
    pallas_call x1, Pallas kernels, on_device(): pl.pallas_call(functools.partial(kernel, heads), out_shape=pltpu.VMEM((co...  75.6 us

profile of v4, /device:TPU:102, one launch (start us, length us, event | category | flops | bytes accessed | tf_op | source)
XLA Modules:
  0.0 77.5 jit_solution(1482304101931133987)
XLA Ops:
  1.3 75.6 %attention_and_output.1 = bf16[112,256]{1,0:T(8,128)(2,1)S(1)} custom-call(s32[1]{0:T(128)S(6)} %copy.15.lengths, s32[1]{0:T(128)S(6)} %copy.16.offset, bf16[32,1024]{1,0:T(8,128)(2,1)} %q_nope_any.1, bf16[32,512]{1,0:T(8,128)(2,1)} %q_rope_any.1, bf16[32,512]{1,0:T(8,128)(2,1)} %prefix_latent.1, bf16[32,64]{1,0:T(8,128)(2,1)} %prefix_rope_any.1, ...), custom_call_target="tpu_custom_call" | custom-call | tf_op jit(solution)/shard_map/attention_and_output/pallas_call | solution.py:747
  76.9 0.6 copy.14

commit v5 on v3

--- a/solution.py
+++ b/solution.py
@@ -225,6 +225,7 @@
     shares,
     arrived,
     passed,
+    own_part,
     q_nope,
     q_rope,
     prefix_rope,
@@ -282,20 +283,6 @@
     served = [jnp.where(place.head == 0, heads - 1 - j, j) for j in range(half_heads)]
     peers = plane_peers(place) + others + [place.across(far_end)]
 
-    greet(peers)
-
-    @pl.when(stays)
-    def _():
-        greet(legs)
-
-    @pl.when(moves)
-    def _():
-        greet([swap_device, swap_across])
-
-    @pl.when(is_end)
-    def _():
-        greet([place.across(head) for head in served])
-
     loads = [
         pltpu.make_async_copy(src, dst, load_sem.at[i])
         for i, (src, dst) in enumerate(
@@ -315,8 +302,27 @@
             )
         )
     ]
-    for load in loads:
-        load.start()
+    early = (9, 4, 5, 0, 1, 10, 11)
+    greet(peers[:7])
+    for i in early:
+        loads[i].start()
+    greet(peers[7:])
+
+    @pl.when(stays)
+    def _():
+        greet(legs)
+
+    @pl.when(moves)
+    def _():
+        greet([swap_device, swap_across])
+
+    @pl.when(is_end)
+    def _():
+        greet([place.across(head) for head in served])
+
+    for i, load in enumerate(loads):
+        if i not in early:
+            load.start()
     lane = lax.broadcasted_iota(jnp.int32, (rows, 128), 1)
     row = lax.broadcasted_iota(jnp.int32, (rows, 128), 0)
     for i in (9, 4, 5):
@@ -480,10 +486,12 @@
     loads[7].wait()
     latent_out = (accum[...] / jnp.sum(row_sum[...], axis=1, keepdims=True)).astype(jnp.bfloat16)
     per_kind = half // VD
-    for head in range(h_dev):
-        staged[head // per_kind, :, pl.ds((head % per_kind) * VD, VD)] = jnp.dot(
-            latent_out[head * rows : (head + 1) * rows], w_uv[head], preferred_element_type=jnp.float32
-        ).astype(jnp.bfloat16)
+
+    def head_outputs(kind):
+        for head in range(kind * per_kind, (kind + 1) * per_kind):
+            staged[kind, :, pl.ds((head % per_kind) * VD, VD)] = jnp.dot(
+                latent_out[head * rows : (head + 1) * rows], w_uv[head], preferred_element_type=jnp.float32
+            ).astype(jnp.bfloat16)
 
     slot = (place.x, place.y, place.core)
     new_slot = (place.x, place.y, 1 - place.core)
@@ -529,19 +537,21 @@
             device_id_type=MESH,
         )
 
-    @pl.when(stays)
-    def _():
-        for kind in (0, 1):
+    for kind in (0, 1):
+        head_outputs(kind)
+
+        @pl.when(stays)
+        def _():
             leg(kind).start()
-        for kind in (0, 1):
             outs[(kind, place.zh) + slot] = staged[kind]
+
+        @pl.when(moves)
+        def _():
+            swap(kind).start()
+            direct(kind).start()
 
     @pl.when(moves)
     def _():
-        for kind in (0, 1):
-            swap(kind).start()
-        for kind in (0, 1):
-            direct(kind).start()
         for kind in (0, 1):
             swap(kind).wait_recv()
 
@@ -588,21 +598,23 @@
             device_id_type=MESH,
         )
 
-    def part_share(zh, plane):
-        total = jnp.zeros((NX * block, w_out.shape[1]), jnp.float32)
+    def part_share(zh, plane, first, count):
+        total = jnp.zeros((count * block, w_out.shape[1]), jnp.float32)
         for kind in (0, 1):
-            tokens = outs[kind, zh, :, :, plane].reshape(NX * block, half)
+            tokens = outs[kind, zh, pl.ds(first, count), :, plane].reshape(count * block, half)
             total = total + last_dims(tokens, w_out[plane, :, kind * half : (kind + 1) * half])
         return total
 
     def send_shares(plane):
         zh = spread.zh(plane)
-        total = part_share(zh, place.core)
+        own_part[...] = part_share(zh, place.core, 0, NX)
         spread.from_sibling(plane)
-        total = total + part_share(zh, 1 - place.core)
         for x in range(NX):
             target = zh * NX + x
-            shares[target] = total[x * block : (x + 1) * block].T.astype(jnp.bfloat16)
+            if x % 2 == 0:
+                total = part_share(zh, 1 - place.core, x, 2)
+                total = total + own_part[x * block : (x + 2) * block]
+            shares[target] = total[x % 2 * block : (x % 2 + 1) * block].T.astype(jnp.bfloat16)
 
             @pl.when(jnp.logical_and(my_quad == zh, target != place.head))
             def _():
@@ -763,6 +775,7 @@
             pltpu.VMEM((heads, columns, block), jnp.bfloat16),
             pltpu.VMEM((heads // 2 + 2, columns, block), jnp.bfloat16),
             pltpu.VMEM((NX, columns, block), jnp.bfloat16),
+            pltpu.VMEM((NX * block, columns), jnp.float32),
             pltpu.VMEM(q_nope.shape, jnp.bfloat16),
             pltpu.VMEM(q_rope.shape, jnp.bfloat16),
             pltpu.VMEM(prefix_rope.shape, jnp.bfloat16),

time: 76.1 us -> 76.1 us (level)
  the two profiles are of different devices: /device:TPU:64 before, /device:TPU:112 now
where the time goes in v5:
time: 76.1 us; the launch traced here: 75.9 us
  Pallas kernels  74 us (97%)
  between operations  1.3 us (2%)
    pallas_call x1, Pallas kernels, on_device(): pl.pallas_call(functools.partial(kernel, heads), out_shape=pltpu.VMEM((co...  74 us

profile of v5, /device:TPU:112, one launch (start us, length us, event | category | flops | bytes accessed | tf_op | source)
XLA Modules:
  0.0 75.9 jit_solution(7367325180421518573)
XLA Ops:
  1.3 74.0 %attention_and_output.1 = bf16[112,256]{1,0:T(8,128)(2,1)S(1)} custom-call(s32[1]{0:T(128)S(6)} %copy.15.lengths, s32[1]{0:T(128)S(6)} %copy.16.offset, bf16[32,1024]{1,0:T(8,128)(2,1)} %q_nope_any.1, bf16[32,512]{1,0:T(8,128)(2,1)} %q_rope_any.1, bf16[32,512]{1,0:T(8,128)(2,1)} %prefix_latent.1, bf16[32,64]{1,0:T(8,128)(2,1)} %prefix_rope_any.1, ...), custom_call_target="tpu_custom_call" | custom-call | tf_op jit(solution)/shard_map/attention_and_output/pallas_call | solution.py:759
  75.3 0.6 copy.14

commit v6 on v5

--- a/solution.py
+++ b/solution.py
@@ -605,9 +605,11 @@
             total = total + last_dims(tokens, w_out[plane, :, kind * half : (kind + 1) * half])
         return total
 
+    def own_share(plane):
+        own_part[...] = part_share(spread.zh(plane), place.core, 0, NX)
+
     def send_shares(plane):
         zh = spread.zh(plane)
-        own_part[...] = part_share(zh, place.core, 0, NX)
         spread.from_sibling(plane)
         for x in range(NX):
             target = zh * NX + x
@@ -637,9 +639,9 @@
                 far_share(target).start()
 
     spread.spread(0)
-    gather.finish(1)
     spread.hand_on(0)
     spread.hand_over(0)
+    gather.finish(1)
     for kind in (0, 1):
         direct(kind).wait_recv()
     spread.start(1)
@@ -647,12 +649,14 @@
     spread.spread(1)
     loads[8].wait()
     w_copy.wait_recv()
-    send_shares(0)
+    own_share(0)
     spread.hand_on(1, (0, 1))
     spread.hand_on(1, (2, 3))
     spread.hand_over(1)
+    send_shares(0)
+    spread.complete(1)
+    own_share(1)
     forward_shares(0)
-    spread.complete(1)
     send_shares(1)
     forward_shares(1)
     spread.finish(0)

time: 76.1 us -> 76.5 us (level)
  the two profiles are of different devices: /device:TPU:112 before, /device:TPU:6 now
where the time goes in v6:
time: 76.5 us; the launch traced here: 76.3 us
  Pallas kernels  74.4 us (97%)
  between operations  1.3 us (2%)
    pallas_call x1, Pallas kernels, on_device(): pl.pallas_call(functools.partial(kernel, heads), out_shape=pltpu.VMEM((co...  74.4 us

profile of v6, /device:TPU:6, one launch (start us, length us, event | category | flops | bytes accessed | tf_op | source)
XLA Modules:
  0.0 76.3 jit_solution(4979658364509411714)
XLA Ops:
  1.3 74.4 %attention_and_output.1 = bf16[112,256]{1,0:T(8,128)(2,1)S(1)} custom-call(s32[1]{0:T(128)S(6)} %copy.15.lengths, s32[1]{0:T(128)S(6)} %copy.16.offset, bf16[32,1024]{1,0:T(8,128)(2,1)} %q_nope_any.1, bf16[32,512]{1,0:T(8,128)(2,1)} %q_rope_any.1, bf16[32,512]{1,0:T(8,128)(2,1)} %prefix_latent.1, bf16[32,64]{1,0:T(8,128)(2,1)} %prefix_rope_any.1, ...), custom_call_target="tpu_custom_call" | custom-call | tf_op jit(solution)/shard_map/attention_and_output/pallas_call | solution.py:763
  75.7 0.6 copy.14

commit v7 on v3

--- a/solution.py
+++ b/solution.py
@@ -46,11 +46,6 @@
 
     def across(self, head=None):
         return (self.ctx(zh=1 - self.zh), self.head if head is None else head)
-
-
-    def up(self, step):
-        z = lax.rem(self.zh * self.heads + self.head + step + 2 * self.heads, 2 * self.heads)
-        return lax.div(z, self.heads), lax.rem(z, self.heads)
 
 
 def greet(devices):
@@ -220,7 +215,6 @@
     accum,
     outs,
     staged,
-    passing,
     w_out,
     shares,
     arrived,
@@ -243,8 +237,6 @@
     o_ring_recv,
     o_pair_send,
     o_pair_recv,
-    leg_send,
-    leg_recv,
     o_cross_send,
     o_cross_recv,
     swap_send,
@@ -270,11 +262,6 @@
     moves = place.core != odd
     is_end = jnp.logical_or(place.head == 0, place.head == heads - 1)
 
-    quarter = heads // 2
-    legs = []
-    for step in (quarter, -quarter):
-        leg_zh, leg_head = place.up(step)
-        legs.append((place.ctx(zh=leg_zh), leg_head))
     swap_device = (place.ctx(core=1 - place.core), paired)
     swap_across = (place.ctx(zh=1 - place.zh, core=1 - place.core), paired)
     others = [(me, lax.rem(place.head + j, heads)) for j in range(1, heads)]
@@ -286,7 +273,7 @@
 
     @pl.when(stays)
     def _():
-        greet(legs)
+        greet([place.across(), place.across()])
 
     @pl.when(moves)
     def _():
@@ -488,24 +475,13 @@
     slot = (place.x, place.y, place.core)
     new_slot = (place.x, place.y, 1 - place.core)
 
-    def leg(kind):
+    def stay(kind):
         return pltpu.make_async_remote_copy(
             src_ref=staged.at[kind],
-            dst_ref=passing.at[kind],
-            send_sem=leg_send.at[kind],
-            recv_sem=leg_recv.at[kind],
-            device_id=legs[kind],
-            device_id_type=MESH,
-        )
-
-    def second_leg(kind):
-        end_zh = place.up(quarter if kind == 0 else -quarter)[0]
-        return pltpu.make_async_remote_copy(
-            src_ref=passing.at[kind],
-            dst_ref=outs.at[(kind, 1 - end_zh) + slot],
+            dst_ref=outs.at[(kind, place.zh) + slot],
             send_sem=o_cross_send.at[kind],
             recv_sem=o_cross_recv.at[kind],
-            device_id=legs[kind],
+            device_id=place.across(),
             device_id_type=MESH,
         )
 
@@ -532,7 +508,7 @@
     @pl.when(stays)
     def _():
         for kind in (0, 1):
-            leg(kind).start()
+            stay(kind).start()
         for kind in (0, 1):
             outs[(kind, place.zh) + slot] = staged[kind]
 
@@ -548,12 +524,6 @@
     spread = Gather(place, outs, o_ring_send, o_ring_recv, o_pair_send, o_pair_recv)
     spread.start(0)
     gather.finish(0)
-
-    @pl.when(stays)
-    def _():
-        for kind in (0, 1):
-            leg(kind).wait_recv()
-            second_leg(kind).start()
 
     block = shares.shape[-1]
 
@@ -682,8 +652,7 @@
     @pl.when(stays)
     def _():
         for kind in (0, 1):
-            leg(kind).wait_send()
-            second_leg(kind).wait_send()
+            stay(kind).wait_send()
 
     @pl.when(moves)
     def _():
@@ -758,7 +727,6 @@
             pltpu.VMEM((q_rows, lat), jnp.float32),
             pltpu.VMEM((2, 2, NX, NY, 2, rows, half), jnp.bfloat16),
             pltpu.VMEM((2, rows, half), jnp.bfloat16),
-            pltpu.VMEM((2, rows, half), jnp.bfloat16),
             pltpu.VMEM((2, columns, 2 * half), jnp.bfloat16),
             pltpu.VMEM((heads, columns, block), jnp.bfloat16),
             pltpu.VMEM((heads // 2 + 2, columns, block), jnp.bfloat16),
@@ -775,7 +743,7 @@
         + gather_scratch()
         + [dma((heads,)), dma((2,))]
         + gather_scratch()
-        + [dma((2,)), dma((2,)), dma((2,)), dma((2,)), dma((2,)), dma((2,))]
+        + [dma((2,)), dma((2,)), dma((2,)), dma((2,))]
         + [dma(()), dma(()), dma((heads,)), dma((heads // 2 + 2,)), dma((NX,)), dma((NX,))],
         compiler_params=pltpu.CompilerParams(
             collective_id=0, has_side_effects=True, vmem_limit_bytes=60 * 1024 * 1024

time: 76.1 us -> 78.5 us (1.032)
  the two profiles are of different devices: /device:TPU:64 before, /device:TPU:97 now
where the time goes in v7:
time: 78.5 us; the launch traced here: 78.4 us
  Pallas kernels  76.5 us (97%)
  between operations  1.3 us (2%)
    pallas_call x1, Pallas kernels, on_device(): pl.pallas_call(functools.partial(kernel, heads), out_shape=pltpu.VMEM((co...  76.5 us

profile of v7, /device:TPU:97, one launch (start us, length us, event | category | flops | bytes accessed | tf_op | source)
XLA Modules:
  0.0 78.4 jit_solution(11597362918205891543)
XLA Ops:
  1.3 76.5 %attention_and_output.1 = bf16[112,256]{1,0:T(8,128)(2,1)S(1)} custom-call(s32[1]{0:T(128)S(6)} %copy.15.lengths, s32[1]{0:T(128)S(6)} %copy.16.offset, bf16[32,1024]{1,0:T(8,128)(2,1)} %q_nope_any.1, bf16[32,512]{1,0:T(8,128)(2,1)} %q_rope_any.1, bf16[32,512]{1,0:T(8,128)(2,1)} %prefix_latent.1, bf16[32,64]{1,0:T(8,128)(2,1)} %prefix_rope_any.1, ...), custom_call_target="tpu_custom_call" | custom-call | tf_op jit(solution)/shard_map/attention_and_output/pallas_call | solution.py:716
  77.8 0.6 copy.14

commit v8 on v3

--- a/solution.py
+++ b/solution.py
@@ -603,6 +603,9 @@
         for x in range(NX):
             target = zh * NX + x
             shares[target] = total[x * block : (x + 1) * block].T.astype(jnp.bfloat16)
+        for i in range(NX):
+            x = jnp.where(zh == 0, i, NX - 1 - i)
+            target = zh * NX + x
 
             @pl.when(jnp.logical_and(my_quad == zh, target != place.head))
             def _():
@@ -617,7 +620,8 @@
 
         @pl.when(jnp.logical_and(my_quad != zh, inner))
         def _():
-            for x in range(NX):
+            for i in range(NX):
+                x = jnp.where(zh == 0, i, NX - 1 - i)
                 target = zh * NX + x
                 hop(target, x).wait_recv()
                 total = shares[target].astype(jnp.float32) + passed[x].astype(jnp.float32)

time: 76.1 us -> 76.9 us (1.011)
  the two profiles are of different devices: /device:TPU:64 before, /device:TPU:145 now
where the time goes in v8:
time: 76.9 us; the launch traced here: 76.8 us
  Pallas kernels  74.8 us (97%)
  between operations  1.3 us (2%)
    pallas_call x1, Pallas kernels, on_device(): pl.pallas_call(functools.partial(kernel, heads), out_shape=pltpu.VMEM((co...  74.8 us

profile of v8, /device:TPU:145, one launch (start us, length us, event | category | flops | bytes accessed | tf_op | source)
XLA Modules:
  0.0 76.8 jit_solution(10595490416689227029)
XLA Ops:
  1.3 74.8 %attention_and_output.1 = bf16[112,256]{1,0:T(8,128)(2,1)S(1)} custom-call(s32[1]{0:T(128)S(6)} %copy.15.lengths, s32[1]{0:T(128)S(6)} %copy.16.offset, bf16[32,1024]{1,0:T(8,128)(2,1)} %q_nope_any.1, bf16[32,512]{1,0:T(8,128)(2,1)} %q_rope_any.1, bf16[32,512]{1,0:T(8,128)(2,1)} %prefix_latent.1, bf16[32,64]{1,0:T(8,128)(2,1)} %prefix_rope_any.1, ...), custom_call_target="tpu_custom_call" | custom-call | tf_op jit(solution)/shard_map/attention_and_output/pallas_call | solution.py:751
  76.1 0.6 copy.14
